TPU v7x, 32 devices: a whole 2x2x4 slice. The times are simulated.
32 devices in a mesh: tm: 4 (over y, x), gx: 4 (over z), gy: 2 (over core).
Axes of the slice: x: 2, y: 2, z: 4, core: 2. Of those that a mesh axis runs over, the one named last changes fastest.
Arguments:
- slice_starts: float32 [4, 64, 32, 256], P('tm', 'gx', 'gy'), may hold values from -2.5 to 4, as said below
- material: int32 [64, 32, 256], P('gx', 'gy'), may hold values from 0 to 7
- conduct_table: float32 [8], replicated, may hold values from 0.5 to 1
- wall_flags: int32 [2, 64, 32], P(None, 'gx', 'gy'), may hold values 0 or 1
- pod_basis: bfloat16 [128, 64, 32, 256], P('tm', 'gx', 'gy'), may hold values from -0.0078125 to 0.0078125
Outputs:
- slice_ends: float32 [4, 64, 32, 256], P('tm', 'gx', 'gy')
- pod_coeffs: float32 [4, 128], P(None, 'tm')
Inputs may be any that keep to these rules, and one draw needn't show every extreme that they name: `slice_starts`: start temperatures.
All inputs are finite; a program needn't handle non-finite values. No bound on the sum of `wall_flags` on one device may be relied on, other than what follows from the above.
Results may differ from a plain program's by a relative error of at most 0.0003.
Values may be sent and summed in bfloat16 or wider, within the bound.
A program may use at most 64 MiB of HBM per device.

v0:
```python
import functools

import jax
import jax.numpy as jnp
from jax import lax
from jax.experimental import pallas as pl
from jax.experimental.pallas import tpu as pltpu
from jax.sharding import PartitionSpec as P

STEPS = 8
W = 4
YP = 8

fine_rate = 0.1
coarse_rate = 0.05

MESH = pl.DeviceIdType.MESH
F32 = jnp.float32
HIGH = lax.Precision.HIGHEST
AROUND = [(a, b) for a in (-1, 0, 1) for b in (-1, 0, 1) if (a, b) != (0, 0)]


def conduct(k_here, k_there):
    bottom = jnp.maximum(k_here + k_there, 1.0)
    return k_here * k_there * pl.reciprocal(bottom, approx=True)


def conduct_exact(k_here, k_there):
    return k_here * k_there / jnp.maximum(k_here + k_there, 1.0)


def iota(shape, dim):
    return lax.broadcasted_iota(jnp.int32, shape, dim)


def mm(a, b):
    return lax.dot_general(a, b, (((1,), (0,)), ((), ())), precision=HIGH, preferred_element_type=F32)


def kernel(sizes, start, material, table, walls, out, means,
           A, B, C, S, SA, KG, K, h_send, h_recv):
    nt, ngx, ngy = sizes
    bx, by, nz = material.shape
    ex, ey = bx + 2 * W, by + 2 * YP
    cx, cy = bx // 4, by // 4
    crows = cx * cy
    t, gx, gy = lax.axis_index("tm"), lax.axis_index("gx"), lax.axis_index("gy")

    def exists(a, b):
        ok = None
        for d, g, n in ((a, gx, ngx), (b, gy, ngy)):
            if d:
                this = (g + d >= 0) & (g + d < n)
                ok = this if ok is None else ok & this
        return ok

    def if_there(a, b, extra=None):
        ok = exists(a, b)
        if extra is not None:
            ok = extra if ok is None else ok & extra
        return pl.when(ok) if ok is not None else (lambda f: f())

    barrier = pltpu.get_barrier_semaphore()
    for a, b in AROUND:
        @if_there(a, b)
        def _():
            pl.semaphore_signal(barrier, inc=1, device_id={"tm": t, "gx": gx + a, "gy": gy + b}, device_id_type=MESH)

    for a, xs in ((-1, slice(0, W)), (1, slice(W + bx, ex))):
        @pl.when(jnp.logical_not(exists(a, 0)))
        def _():
            for ref in (A, C, S):
                ref[xs] = jnp.zeros((W, ey, nz), F32)
    for b, ys in ((-1, slice(0, YP)), (1, slice(YP + by, ey))):
        @pl.when(jnp.logical_not(exists(0, b)))
        def _():
            for ref in (A, C, S):
                ref[:, ys, :] = jnp.zeros((ex, YP, nz), F32)
    lane = iota((by, nz), 1)
    eye = iota((by, by), 0) == iota((by, by), 1)

    @pl.loop(0, bx)
    def _(x):
        mat = material[x]
        coef = jnp.zeros((by, nz), F32)
        for region in range(table.shape[0]):
            coef = jnp.where(mat == region, table[region], coef)
        low = jnp.sum(jnp.where(eye, walls[0, pl.ds(x, 1), :].astype(F32), 0.0), axis=1, keepdims=True)
        top = jnp.sum(jnp.where(eye, walls[1, pl.ds(x, 1), :].astype(F32), 0.0), axis=1, keepdims=True)
        flag = jnp.where(lane == 0, low, jnp.where(lane == nz - 1, top, 0.0))
        S[W + x, YP:YP + by, :] = jnp.where(flag > 0.5, -coef, coef)
        A[W + x, YP:YP + by, :] = start[0, x]

    rows_p = (cx * cy, cx * by)
    gather_rows = jnp.where(
        (iota(rows_p, 0) // cy == iota(rows_p, 1) // by) & (iota(rows_p, 0) % cy == (iota(rows_p, 1) % by) // 4), 1.0, 0.0)
    gather_lanes = jnp.where(iota((nz, 128), 0) // 4 == iota((nz, 128), 1), 1.0 / 64.0, 0.0)
    def restrict(cell):
        slabs = []
        for X in range(cx):
            slabs.append((cell(4 * X) + cell(4 * X + 1)) + (cell(4 * X + 2) + cell(4 * X + 3)))
        return mm(mm(gather_rows, jnp.concatenate(slabs, axis=0)), gather_lanes)

    pl.semaphore_wait(barrier, (1 + (gx > 0).astype(jnp.int32) + (gx < ngx - 1).astype(jnp.int32))
                      * (1 + (gy > 0).astype(jnp.int32) + (gy < ngy - 1).astype(jnp.int32)) - 1)

    def halo(ref, kind, i, a, b):
        xs = {-1: (W, W + bx, W), 0: (W, W, bx), 1: (bx, 0, W)}[a]
        ys = {-1: (YP, YP + by, YP), 0: (YP, YP, by), 1: (by, 0, YP)}[b]
        return pltpu.make_async_remote_copy(
            src_ref=ref.at[pl.ds(xs[0], xs[2]), pl.ds(ys[0], ys[2]), :],
            dst_ref=ref.at[pl.ds(xs[1], xs[2]), pl.ds(ys[1], ys[2]), :],
            send_sem=h_send.at[kind, i],
            recv_sem=h_recv.at[kind, i],
            device_id={"tm": t, "gx": gx + a, "gy": gy + b},
            device_id_type=MESH,
        )

    def send_halo(ref, kind):
        for i, (a, b) in enumerate(AROUND):
            @if_there(a, b)
            def _():
                halo(ref, kind, i, a, b).start()

    def left_halo(ref, kind):
        for i, (a, b) in enumerate(AROUND):
            @if_there(a, b)
            def _():
                halo(ref, kind, i, a, b).wait_send()

    def land_halo(ref, kind):
        for i, (a, b) in enumerate(AROUND):
            @if_there(-a, -b)
            def _():
                xs = {-1: (W + bx, W), 0: (W, bx), 1: (0, W)}[a]
                ys = {-1: (YP + by, YP), 0: (YP, by), 1: (0, YP)}[b]
                spot = ref.at[pl.ds(xs[0], xs[1]), pl.ds(ys[0], ys[1]), :]
                pltpu.make_async_remote_copy(
                    src_ref=spot, dst_ref=spot, send_sem=h_send.at[kind, i], recv_sem=h_recv.at[kind, i],
                    device_id={"tm": t, "gx": gx - a, "gy": gy - b}, device_id_type=MESH,
                ).wait_recv()

    send_halo(A, 0)
    send_halo(S, 1)

    own = slice(YP, YP + by)
    means[0:crows, :] = restrict(lambda x: A[W + x, own, :])
    means[crows:2 * crows, :] = restrict(lambda x: jnp.abs(S[W + x, own, :]))

    def conductivity(src, r):
        @pl.loop(W - r - 1, W + bx + r + 1)
        def _(x):
            K[x] = SA[x] * (1.0 + 0.5 * jnp.tanh(src[x]))

    def step(src, put, r):
        conductivity(src, r)
        ylo, yhi = (YP, YP + by) if r == 0 else (YP - 4, YP + by + 4)
        rows = slice(ylo, yhi)
        last = iota((yhi - ylo, nz), 1) == nz - 1

        def body(x, carry):
            kc, uc, fxm = carry
            kn, un = K[x + 1, rows, :], src[x + 1, rows, :]
            fx = conduct(kc, kn) * (un - uc)
            total = fx - fxm
            total += conduct(kc, K[x, ylo + 1:yhi + 1, :]) * (src[x, ylo + 1:yhi + 1, :] - uc)
            total += conduct(kc, K[x, ylo - 1:yhi - 1, :]) * (src[x, ylo - 1:yhi - 1, :] - uc)
            fz = conduct(kc, pltpu.roll(kc, nz - 1, 1)) * (pltpu.roll(uc, nz - 1, 1) - uc)
            fz = jnp.where(last, 0.0, fz)
            total += fz - pltpu.roll(fz, 1, 1)
            total -= conduct(kc, KG[x, rows, :]) * uc
            put(x, rows, uc + (2.0 * fine_rate) * total)
            return kn, un, fx

        x0 = W - r
        k0, u0 = K[x0, rows, :], src[x0, rows, :]
        k1, u1 = K[x0 - 1, rows, :], src[x0 - 1, rows, :]
        lax.fori_loop(x0, W + bx + r, body, (k0, u0, conduct(k0, k1) * (u0 - u1)))

    def into(ref):
        def put(x, rows, value):
            ref[x, rows, :] = value
        return put

    def into_out(x, rows, value):
        out[0, x - W] = value

    land_halo(A, 0)
    land_halo(S, 1)

    @pl.loop(0, ex)
    def _(x):
        s = S[x]
        SA[x] = jnp.abs(s)
        KG[x] = jnp.where(s < 0.0, -s, 0.0)

    def exchange_then(src, kind):
        send_halo(src, kind)
        land_halo(src, kind)

    step(A, into(B), 3)
    left_halo(A, 0)
    step(B, into(A), 2)
    step(A, into(B), 1)
    step(B, into(C), 0)
    exchange_then(C, 2)
    step(C, into(B), 3)
    step(B, into(A), 2)
    step(A, into(B), 1)

    step(B, into_out, 0)
    means[2 * crows:, :] = restrict(lambda x: out[0, x])
    left_halo(S, 1)
    left_halo(C, 2)


def finish(cy, ends, change, out):
    bx, by, nz = ends.shape[1:]
    cx = bx // 4
    shape = (cx * by, cx * cy)
    spread_rows = jnp.where(
        (iota(shape, 1) // cy == iota(shape, 0) // by) & (iota(shape, 1) % cy == (iota(shape, 0) % by) // 4), 1.0, 0.0)
    spread_lanes = jnp.where(iota((nz // 4, nz), 1) // 4 == iota((nz // 4, nz), 0), 1.0, 0.0)
    wide = mm(mm(spread_rows, change[...]), spread_lanes)
    for x in range(bx):
        X = x // 4
        out[0, x] = ends[0, x] + wide[X * by:(X + 1) * by, :]


def project(ends, basis, coeffs, acc):
    nt, bx = ends.shape[0], ends.shape[1]
    modes = basis.shape[0]
    for n in range(nt):
        for base in range(0, modes, 16):
            def body(x, carry):
                u = ends[n, x]
                new = []
                for j in range(16):
                    p = basis[base + j, x].astype(F32) * u
                    p = (p[0:8, 0:128] + p[0:8, 128:256]) + (p[8:16, 0:128] + p[8:16, 128:256])
                    new.append(carry[j] + p)
                return tuple(new)
            sums = lax.fori_loop(0, bx, body, tuple(jnp.zeros((8, 128), F32) for _ in range(16)))
            for j in range(16):
                acc[n * modes + base + j:n * modes + base + j + 1, :] = jnp.sum(sums[j], axis=0, keepdims=True)
    ones = jnp.ones((8, 128), F32)
    coeffs[...] = lax.dot_general(ones, acc[...], (((1,), (1,)), ((), ())), precision=HIGH, preferred_element_type=F32)


def coarse_step(c, k0):
    k = k0 * (1.0 + 0.5 * jnp.tanh(c))
    total = jnp.zeros_like(c)
    for dim in range(3):
        n = c.shape[dim]
        ka, kb = lax.slice_in_dim(k, 0, n - 1, axis=dim), lax.slice_in_dim(k, 1, n, axis=dim)
        f = conduct_exact(ka, kb) * (lax.slice_in_dim(c, 1, n, axis=dim) - lax.slice_in_dim(c, 0, n - 1, axis=dim))
        after = [(0, 0)] * 3
        before = [(0, 0)] * 3
        after[dim], before[dim] = (0, 1), (1, 0)
        total += jnp.pad(f, after) - jnp.pad(f, before)
    return c + (2.0 * coarse_rate) * total


def local(sizes, slice_starts, material, conduct_table, wall_flags, pod_basis):
    nt, ngx, ngy = sizes
    bx, by, nz = material.shape
    modes = pod_basis.shape[0]
    cx, cy, cz = bx // 4, by // 4, nz // 4
    crows = cx * cy
    extended = pltpu.VMEM((bx + 2 * W, by + 2 * YP, nz), F32)
    dma = pltpu.SemaphoreType.DMA
    vmem = pl.BlockSpec(memory_space=pltpu.VMEM)
    fine_end, means = pl.pallas_call(
        functools.partial(kernel, sizes),
        out_shape=(jax.ShapeDtypeStruct(slice_starts.shape, F32), jax.ShapeDtypeStruct((3 * crows, 128), F32)),
        in_specs=[vmem, vmem, pl.BlockSpec(memory_space=pltpu.SMEM), vmem],
        out_specs=(vmem, vmem),
        scratch_shapes=[extended] * 7 + [dma((3, 8)), dma((3, 8))],
        compiler_params=pltpu.CompilerParams(collective_id=0, has_side_effects=True, vmem_limit_bytes=32 * 1024 * 1024),
    )(slice_starts, material, conduct_table, wall_flags)
    every = lax.all_gather(means, ("tm", "gx", "gy"), axis=0, tiled=False)
    every = every.reshape(nt, ngx, ngy, 3, cx, cy, 128)[..., :cz]
    every = every.transpose(3, 0, 1, 4, 2, 5, 6).reshape(3, nt, ngx * cx, ngy * cy, cz)
    coef = every[1, 0]
    starts = every[0]
    moved = jax.vmap(lambda c: coarse_step(c, coef))(starts)
    current = starts[0]
    changes = []
    for n in range(nt):
        ahead = coarse_step(current, coef)
        changes.append(ahead - moved[n])
        current = changes[n] + every[2, n]
    t, gx, gy = lax.axis_index("tm"), lax.axis_index("gx"), lax.axis_index("gy")
    change = lax.dynamic_slice(jnp.stack(changes), (t, gx * cx, gy * cy, 0), (1, cx, cy, cz)).reshape(crows, cz)
    ends = pl.pallas_call(
        functools.partial(finish, cy),
        out_shape=jax.ShapeDtypeStruct(slice_starts.shape, F32),
        in_specs=[vmem, vmem],
        out_specs=vmem,
    )(fine_end, change)
    gathered = lax.all_gather(ends, "tm", axis=0, tiled=True)
    sums = pl.pallas_call(
        project,
        out_shape=jax.ShapeDtypeStruct((8, nt * modes), F32),
        in_specs=[vmem, vmem],
        out_specs=vmem,
        scratch_shapes=[pltpu.VMEM((nt * modes, 128), F32)],
        compiler_params=pltpu.CompilerParams(vmem_limit_bytes=32 * 1024 * 1024),
    )(gathered, pod_basis)
    return ends, lax.psum(sums[0].reshape(nt, modes), ("gx", "gy"))


def solution(mesh):
    in_specs = (
        P("tm", "gx", "gy", None),
        P("gx", "gy", None),
        P(),
        P(None, "gx", "gy"),
        P("tm", "gx", "gy", None),
    )
    out_specs = (P("tm", "gx", "gy", None), P(None, "tm"))
    sizes = tuple(mesh.shape[name] for name in ("tm", "gx", "gy"))
    return jax.shard_map(functools.partial(local, sizes), mesh=mesh, in_specs=in_specs, out_specs=out_specs, check_vma=False)
```

profile of v0, /device:TPU:0, one launch (start us, length us, event | category | flops | bytes accessed | tf_op | source)
XLA Modules:
  0.0 157.1 jit_solution(7964034190739882226)
XLA Ops:
  7.2 0.0 all-gather.3.cloned.1.call-start
  7.2 0.0 copy-start.2
  7.2 0.9 copy-done.2
  8.2 0.9 copy-done.3
  9.1 0.7 copy-done.5
  9.8 0.7 copy-done.6
  10.5 43.3 %shard_map.68 = (f32[1,16,16,256]{3,2,1,0:T(8,128)S(1)}, f32[48,128]{1,0:T(8,128)S(1)}) custom-call(f32[1,16,16,256]{3,2,1,0:T(8,128)S(1)} %copy-done.2, s32[16,16,256]{2,1,0:T(8,128)S(1)} %copy-done.3, f32[8]{0:T(128)S(1)} %copy-done.6, s32[2,16,16]{2,1,0:T(8,128)S(1)} %copy-done.5), custom_call_target="tpu_custom_call" | custom-call | tf_op jit(solution)/shard_map/pallas_call | solution.py:273
  53.8 0.0 copy-start.4
  53.8 43.5 %all-gather = f32[1536,128]{1,0:T(8,128)S(1)} all-gather(f32[48,128]{1,0:T(8,128)S(1)} %get-tuple-element.5), channel_id=2, replica_groups=mesh['tm'=4,'gx'=4,'gy'=2] {'tm','gx','gy'}, dimensions={0}, use_global_device_ids=true | all-gather | bytes 811008 | tf_op jit(solution)/shard_map/all_gather | solution.py:281
  97.3 0.1 slice_bitcast_fusion
  97.4 0.2 copy.11
  97.7 0.1 fusion.17
  98.0 0.1 fusion.2
  98.0 0.2 fusion
  98.3 0.1 fusion.1
  98.4 0.1 multiply_add_fusion
  98.5 0.1 add_multiply_fusion.3
  98.7 0.1 fusion.13
  98.8 0.1 add_multiply_fusion.2
  98.9 0.1 fusion.9
  99.1 0.1 add_multiply_fusion.1
  99.2 0.1 fusion.5
  99.4 0.1 fusion.4
  99.5 0.6 fusion.25
  100.1 2.0 %shard_map.69 = f32[1,16,16,256]{3,2,1,0:T(8,128)} custom-call(f32[1,16,16,256]{3,2,1,0:T(8,128)} %copy-done.4, f32[16,64]{1,0:T(8,128)} %bitcast.77), custom_call_target="tpu_custom_call" | custom-call | tf_op jit(solution)/shard_map/pallas_call | solution.py:295
  102.1 0.0 all-gather.3.cloned.1.call-update
  102.2 23.0 %all-gather.3.cloned.1.call-done.ends = f32[4,16,16,256]{3,2,1,0:T(8,128)} async-done(((f32[1,16,16,256]{3,2,1,0:T(8,128)}), f32[4,16,16,256]{3,2,1,0:T(8,128)}) %all-gather.3.cloned.1.call-update) | async-done | bytes 1048592 | tf_op jit(solution)/shard_map/all_gather | solution.py:301
  125.2 2.2 %copy-done = bf16[32,16,16,256]{3,2,1,0:T(8,128)(2,1)S(1)} copy-done((bf16[32,16,16,256]{3,2,1,0:T(8,128)(2,1)S(1)}, bf16[32,16,16,256]{3,2,1,0:T(8,128)(2,1)}, u32[]{:S(2)}) %copy-start) | copy-done | bytes 4194328
  127.4 1.2 copy-done.1
  128.6 4.6 %shard_map.70 = f32[8,128]{1,0:T(8,128)S(1)} custom-call(f32[4,16,16,256]{3,2,1,0:T(8,128)S(1)} %copy-done.1, bf16[32,16,16,256]{3,2,1,0:T(8,128)(2,1)S(1)} %copy-done), custom_call_target="tpu_custom_call" | custom-call | tf_op jit(solution)/shard_map/pallas_call | solution.py:302
  133.2 0.1 reshape_squeeze.3
  133.3 16.9 %psum.7 = f32[4,32]{1,0:T(4,128)} all-reduce(f32[4,32]{1,0:T(4,128)S(1)} %reshape_squeeze.3), channel_id=1, replica_groups=mesh['tm'=4,'gx'=4,'gy'=2] {'gx','gy'}, use_global_device_ids=true, to_apply=%region_0.1 | all-reduce | flops 128 | bytes 1024 | tf_op jit(solution)/shard_map/psum | solution.py:310
  (22 shorter events, 0.4 us)
Async XLA Ops:
  7.2 118.0 %all-gather.3.cloned.1.call-start = ((), (), s32[]{:S(2)}) async-start(), calls=%async_computation | async-start | bytes 1310720 | tf_op jit(solution)/shard_map/all_gather | solution.py:301
  7.2 1.0 copy-start.2
  8.2 0.9 copy-start.3
  9.1 0.7 copy-start.5
  9.8 0.7 copy-start.6
  53.8 44.5 %copy-start.4 = (f32[1,16,16,256]{3,2,1,0:T(8,128)}, f32[1,16,16,256]{3,2,1,0:T(8,128)S(1)}, u32[]{:S(2)}) copy-start(f32[1,16,16,256]{3,2,1,0:T(8,128)S(1)} %get-tuple-element.4.ends) | copy-start | bytes 786436
  125.2 2.2 %copy-start = (bf16[32,16,16,256]{3,2,1,0:T(8,128)(2,1)S(1)}, bf16[32,16,16,256]{3,2,1,0:T(8,128)(2,1)}, u32[]{:S(2)}) copy-start(bf16[32,16,16,256]{3,2,1,0:T(8,128)(2,1)} %basis.1) | copy-start | bytes 12582916
  127.4 1.2 copy-start.1
Sparse Core Ops, SparseCore 0:
  102.3 22.8 all-gather.2
where the time goes:
time: 157 us
  blocking collectives  60.4 us (38%)
  Pallas kernels  49.9 us (32%)
  waiting for transfers between devices  23 us (15%)
  between operations  14.3 us (9%)
  local copies, waits for them, and re-layouts  7.16 us (5%)
  other arithmetic  2.27 us (1%)
    all_gather x1, blocking collectives, local(): every = lax.all_gather(means, ('tm', 'gx', 'gy'), axis=0, tiled=False)  43.5 us
    pallas_call x1, Pallas kernels, local(): pl.pallas_call(functools.partial(kernel, sizes), out_shape=(jax.ShapeDtyp...  43.3 us
    all_gather x1, waiting for transfers between devices, local(): gathered = lax.all_gather(ends, 'tm', axis=0, tiled=True)  23 us
    psum x1, blocking collectives, local(): return (ends, lax.psum(sums[0].reshape(nt, modes), ('gx', 'gy')))  16.9 us
    unnamed x14, local copies, waits for them, and re-layouts  6.68 us
    pallas_call x1, Pallas kernels, local(): pl.pallas_call(project, out_shape=jax.ShapeDtypeStruct((8, nt * modes), F...  4.58 us
  transfers between devices with their start and end apart: 1, of which 1 were waited for; matrix products, arithmetic and copies ran while one was open for 0% of the time, Pallas kernels for 0%

commit v1 on v0

--- a/solution.py
+++ b/solution.py
@@ -278,9 +278,10 @@
         scratch_shapes=[extended] * 7 + [dma((3, 8)), dma((3, 8))],
         compiler_params=pltpu.CompilerParams(collective_id=0, has_side_effects=True, vmem_limit_bytes=32 * 1024 * 1024),
     )(slice_starts, material, conduct_table, wall_flags)
-    every = lax.all_gather(means, ("tm", "gx", "gy"), axis=0, tiled=False)
-    every = every.reshape(nt, ngx, ngy, 3, cx, cy, 128)[..., :cz]
-    every = every.transpose(3, 0, 1, 4, 2, 5, 6).reshape(3, nt, ngx * cx, ngy * cy, cz)
+    every = lax.all_gather(means, "tm", axis=0, tiled=True)
+    every = lax.all_gather(every, ("gx", "gy"), axis=0, tiled=True)
+    every = every.reshape(ngx, ngy, nt, 3, cx, cy, 128)[..., :cz]
+    every = every.transpose(3, 2, 0, 4, 1, 5, 6).reshape(3, nt, ngx * cx, ngy * cy, cz)
     coef = every[1, 0]
     starts = every[0]
     moved = jax.vmap(lambda c: coarse_step(c, coef))(starts)

time: 157 us -> 141 us (0.90)
  blocking collectives: 60.4 us -> 40.9 us
  waiting for transfers between devices: 23 us -> 25.7 us
    all_gather x1 -> x2, blocking collectives: 43.5 us -> 24 us  [the longest x1 15.6 us: local(): every = lax.all_gather(every, ('gx', 'gy'), axis=0, tiled=True)]
    all_gather x1, waiting for transfers between devices: 23 us -> 25.7 us  [local(): gathered = lax.all_gather(ends, 'tm', axis=0, tiled=True)]
where the time goes in v1:
time: 141 us; the launch traced here: 140 us
  Pallas kernels  49.9 us (35%)
  blocking collectives  40.9 us (29%)
  waiting for transfers between devices  25.7 us (18%)
  between operations  14.3 us (10%)
  local copies, waits for them, and re-layouts  7.17 us (5%)
  other arithmetic  2.26 us (2%)
    pallas_call x1, Pallas kernels, local(): pl.pallas_call(functools.partial(kernel, sizes), out_shape=(jax.ShapeDtyp...  43.3 us
    all_gather x1, waiting for transfers between devices, local(): gathered = lax.all_gather(ends, 'tm', axis=0, tiled=True)  25.7 us
    psum x1, blocking collectives, local(): return (ends, lax.psum(sums[0].reshape(nt, modes), ('gx', 'gy')))  16.9 us
    all_gather x1, blocking collectives, local(): every = lax.all_gather(every, ('gx', 'gy'), axis=0, tiled=True)  15.6 us
    all_gather x1, blocking collectives, local(): every = lax.all_gather(means, 'tm', axis=0, tiled=True)  8.37 us
    unnamed x14, local copies, waits for them, and re-layouts  6.68 us
    pallas_call x1, Pallas kernels, local(): pl.pallas_call(project, out_shape=jax.ShapeDtypeStruct((8, nt * modes), F...  4.58 us
  transfers between devices with their start and end apart: 1, of which 1 were waited for; matrix products, arithmetic and copies ran while one was open for 0% of the time, Pallas kernels for 0%

profile of v1, /device:TPU:0, one launch (start us, length us, event | category | flops | bytes accessed | tf_op | source)
XLA Modules:
  0.0 140.2 jit_solution(14944415950994334711)
XLA Ops:
  7.2 0.0 all-gather.2.cloned.1.call-start
  7.2 0.9 copy-done.2
  8.2 0.9 copy-done.3
  9.1 0.7 copy-done.5
  9.8 0.7 copy-done.6
  10.5 43.3 %shard_map.68 = (f32[1,16,16,256]{3,2,1,0:T(8,128)S(1)}, f32[48,128]{1,0:T(8,128)S(1)}) custom-call(f32[1,16,16,256]{3,2,1,0:T(8,128)S(1)} %copy-done.2, s32[16,16,256]{2,1,0:T(8,128)S(1)} %copy-done.3, f32[8]{0:T(128)S(1)} %copy-done.6, s32[2,16,16]{2,1,0:T(8,128)S(1)} %copy-done.5), custom_call_target="tpu_custom_call" | custom-call | tf_op jit(solution)/shard_map/pallas_call | solution.py:273
  53.8 8.4 %all_gather.9 = f32[192,128]{1,0:T(8,128)S(1)} all-gather(f32[48,128]{1,0:T(8,128)S(1)} %get-tuple-element.5), channel_id=1, replica_groups=mesh['tm'=4,'gx'=4,'gy'=2] {'tm'}, dimensions={0}, use_global_device_ids=true | all-gather | bytes 122880 | tf_op jit(solution)/shard_map/all_gather | solution.py:281
  62.1 15.6 %all_gather.10 = f32[1536,128]{1,0:T(8,128)S(1)} all-gather(f32[192,128]{1,0:T(8,128)S(1)} %all_gather.9), channel_id=1, replica_groups=mesh['tm'=4,'gx'=4,'gy'=2] {'gx','gy'}, dimensions={0}, use_global_device_ids=true | all-gather | bytes 884736 | tf_op jit(solution)/shard_map/all_gather | solution.py:282
  77.8 0.1 slice_bitcast_fusion
  77.9 0.2 copy.11
  78.2 0.1 fusion.17
  78.3 0.1 copy.12
  78.4 0.1 fusion.2
  78.5 0.2 fusion
  78.7 0.1 fusion.1
  78.8 0.1 multiply_add_fusion
  79.0 0.1 add_multiply_fusion.3
  79.1 0.1 fusion.13
  79.3 0.1 add_multiply_fusion.2
  79.4 0.1 fusion.9
  79.6 0.1 add_multiply_fusion.1
  79.7 0.1 fusion.5
  79.9 0.1 fusion.4
  80.0 0.6 fusion.25
  80.6 2.0 %shard_map.69 = f32[1,16,16,256]{3,2,1,0:T(8,128)} custom-call(f32[1,16,16,256]{3,2,1,0:T(8,128)} %copy-done.4, f32[16,64]{1,0:T(8,128)} %bitcast.77), custom_call_target="tpu_custom_call" | custom-call | tf_op jit(solution)/shard_map/pallas_call | solution.py:296
  82.6 0.0 all-gather.2.cloned.1.call-update
  82.7 25.7 %all-gather.2.cloned.1.call-done.ends = f32[4,16,16,256]{3,2,1,0:T(8,128)} async-done(((f32[1,16,16,256]{3,2,1,0:T(8,128)}), f32[4,16,16,256]{3,2,1,0:T(8,128)}) %all-gather.2.cloned.1.call-update) | async-done | bytes 1048592 | tf_op jit(solution)/shard_map/all_gather | solution.py:302
  108.4 2.2 %copy-done = bf16[32,16,16,256]{3,2,1,0:T(8,128)(2,1)S(1)} copy-done((bf16[32,16,16,256]{3,2,1,0:T(8,128)(2,1)S(1)}, bf16[32,16,16,256]{3,2,1,0:T(8,128)(2,1)}, u32[]{:S(2)}) %copy-start) | copy-done | bytes 4194328
  110.5 1.2 copy-done.1
  111.8 4.6 %shard_map.70 = f32[8,128]{1,0:T(8,128)S(1)} custom-call(f32[4,16,16,256]{3,2,1,0:T(8,128)S(1)} %copy-done.1, bf16[32,16,16,256]{3,2,1,0:T(8,128)(2,1)S(1)} %copy-done), custom_call_target="tpu_custom_call" | custom-call | tf_op jit(solution)/shard_map/pallas_call | solution.py:303
  116.4 0.1 reshape_squeeze.3
  116.5 16.9 %psum.7 = f32[4,32]{1,0:T(4,128)} all-reduce(f32[4,32]{1,0:T(4,128)S(1)} %reshape_squeeze.3), channel_id=1, replica_groups=mesh['tm'=4,'gx'=4,'gy'=2] {'gx','gy'}, use_global_device_ids=true, to_apply=%region_0.1 | all-reduce | flops 128 | bytes 1024 | tf_op jit(solution)/shard_map/psum | solution.py:311
  (23 shorter events, 0.4 us)
Async XLA Ops:
  7.2 101.2 %all-gather.2.cloned.1.call-start = ((), (), s32[]{:S(2)}) async-start(), calls=%async_computation | async-start | bytes 1310720 | tf_op jit(solution)/shard_map/all_gather | solution.py:302
  7.2 1.0 copy-start.2
  8.2 0.9 copy-start.3
  9.1 0.7 copy-start.5
  9.8 0.7 copy-start.6
  53.8 24.8 %copy-start.4 = (f32[1,16,16,256]{3,2,1,0:T(8,128)}, f32[1,16,16,256]{3,2,1,0:T(8,128)S(1)}, u32[]{:S(2)}) copy-start(f32[1,16,16,256]{3,2,1,0:T(8,128)S(1)} %get-tuple-element.4.ends) | copy-start | bytes 786436
  108.4 2.2 %copy-start = (bf16[32,16,16,256]{3,2,1,0:T(8,128)(2,1)S(1)}, bf16[32,16,16,256]{3,2,1,0:T(8,128)(2,1)}, u32[]{:S(2)}) copy-start(bf16[32,16,16,256]{3,2,1,0:T(8,128)(2,1)} %basis.1) | copy-start | bytes 12582916
  110.5 1.2 copy-start.1
Sparse Core Ops, SparseCore 0:
  82.8 25.5 all-gather.1
